TPU v7x, 32 devices: a whole 2x2x4 slice. The times are simulated.
32 devices in a mesh: grp: 8 (over z, core), head: 4 (over y, x).
Axes of the slice: x: 2, y: 2, z: 4, core: 2. Of those that a mesh axis runs over, the one named last changes fastest.
Arguments:
- res_cache: bfloat16 [32, 128, 576], P('grp'), may hold values from -6 to 6, as said below
- res_lengths: int32 [32], P('grp'), may hold values from 2 to 128, as said below
- res_query: bfloat16 [32, 16, 576], P('grp', 'head'), may hold values from -40 to 40
- new_cache: bfloat16 [8, 2048, 576], P(None, ('grp', 'head')), may hold values from -6 to 6, as said below
- new_lengths: int32 [8], replicated, may hold values from 2 to 2048, as said below
- assignment: int32 [8], replicated, may hold values from 0 to 7, each once
- new_query: bfloat16 [8, 16, 576], P('grp', 'head'), may hold values from -40 to 40
- value_up_weight: bfloat16 [16, 512, 128], P('head'), may hold values from -1.5 to 1.5
- w_out: bfloat16 [2048, 3584], P('head'), may hold values from -0.125 to 0.125
Outputs:
- res_mixed: bfloat16 [32, 3584], P('grp')
- new_mixed: bfloat16 [8, 3584], P('grp')
Inputs may be any that keep to these rules, and one draw needn't show every extreme that they name: `res_cache`: tokens of a cache may differ in scale. `res_lengths`: at least 2, and some row reaches 128. `new_cache`: tokens of a cache may differ in scale. `new_lengths`: at least 2, and some request reaches 2048. `assignment`: every group serves exactly one request.
All inputs are finite; a program needn't handle non-finite values.
Results may differ from a plain program's by a relative error of at most 0.012.
Values may be sent and summed in bfloat16 or wider, within the bound.
A program may use at most 128 MiB of HBM per device.

v0:
```python
import jax
import jax.numpy as jnp
from jax import lax
from jax.sharding import PartitionSpec as P

score_scale = 192.0 ** (-0.5)
neg_large = -1e30


def per_device(
    res_cache,
    res_lengths,
    res_query,
    new_cache,
    new_lengths,
    assignment,
    new_query,
    value_up_weight,
    w_out,
):
    group_index = lax.axis_index("grp")
    head_count = lax.axis_size("head")
    local_heads = value_up_weight.shape[0]
    kv_width = value_up_weight.shape[1]
    pre_rows = new_cache.shape[1]
    requests = assignment.shape[0]
    group_slots = jnp.arange(requests, dtype=jnp.int32)
    inverse = jnp.sum(
        jnp.where(assignment[:, None] == group_slots[None, :], group_slots[:, None], 0), axis=0
    )
    served_length = new_lengths[inverse[group_index]]
    outgoing = jnp.take(new_cache, inverse, axis=0)
    arrived = lax.all_to_all(outgoing, "grp", split_axis=0, concat_axis=1, tiled=True)[0]
    block_rows = arrived.shape[0]
    token_slots = jnp.arange(res_cache.shape[1], dtype=jnp.int32)
    usable = token_slots[None, :] < res_lengths[:, None]
    scores = (
        jnp.einsum("rhc,rlc->rhl", res_query, res_cache, preferred_element_type=jnp.float32)
        * score_scale
    )
    scores = jnp.where(usable[:, None, :], scores, neg_large)
    running_max = jnp.max(scores, axis=2, keepdims=True)
    attention_weights = jnp.where(usable[:, None, :], jnp.exp(scores - running_max), 0.0)
    weight_sum = jnp.sum(attention_weights, axis=2, keepdims=True)
    res_weighted = jnp.einsum(
        "rhl,rlk->rhk",
        attention_weights.astype(jnp.bfloat16),
        res_cache[:, :, :kv_width],
        preferred_element_type=jnp.float32,
    )
    res_latent = (res_weighted / weight_sum).astype(jnp.bfloat16)
    queries = new_query[0]
    shard_rows = lax.all_gather(arrived, "head", axis=0, tiled=True)
    best = jnp.full((local_heads,), neg_large, jnp.float32)
    token_index = jnp.arange(shard_rows.shape[0], dtype=jnp.int32)
    owner_rank = token_index // block_rows
    source = token_index % block_rows // pre_rows
    position = (source * head_count + owner_rank) * pre_rows + token_index % pre_rows
    valid_rows = position < served_length
    part_scores = (
        lax.dot_general(
            queries, shard_rows, (((1,), (1,)), ((), ())), preferred_element_type=jnp.float32
        )
        * score_scale
    )
    part_scores = jnp.where(valid_rows[None, :], part_scores, neg_large)
    new_best = jnp.maximum(best, jnp.max(part_scores, axis=1))
    part_weights = jnp.where(valid_rows[None, :], jnp.exp(part_scores - new_best[:, None]), 0.0)
    weight_total = jnp.sum(part_weights, axis=1)
    weighted = jnp.dot(
        part_weights.astype(jnp.bfloat16),
        shard_rows[:, :kv_width],
        preferred_element_type=jnp.float32,
    )
    best, weight_total, weighted = (new_best, weight_total, weighted)
    new_latent = (weighted / weight_total[:, None]).astype(jnp.bfloat16)
    joined_latents = jnp.concatenate([res_latent, new_latent[None]], axis=0)
    per_head_values = jnp.einsum(
        "dic,icn->din", joined_latents, value_up_weight, preferred_element_type=jnp.float32
    ).astype(jnp.bfloat16)
    head_rows = per_head_values.reshape(per_head_values.shape[0], -1)
    resident = res_cache.shape[0]
    partial_out = jnp.dot(head_rows, w_out, preferred_element_type=jnp.float32)
    mixed = lax.psum(partial_out.astype(jnp.bfloat16), "head")
    return (mixed[:resident], mixed[resident:])


def solution(mesh):
    in_specs = (
        P("grp", None, None),
        P("grp"),
        P("grp", "head", None),
        P(None, ("grp", "head"), None),
        P(),
        P(),
        P("grp", "head", None),
        P("head", None, None),
        P("head", None),
    )
    out_specs = (P("grp", None), P("grp", None))
    return jax.shard_map(
        per_device, mesh=mesh, in_specs=in_specs, out_specs=out_specs, check_vma=False
    )
```

profile of v0, /device:TPU:0, one launch (start us, length us, event | category | flops | bytes accessed | tf_op | source)
XLA Modules:
  0.0 102.6 jit_solution(3982231848599705459)
XLA Ops:
  7.2 0.0 copy-start
  7.2 0.0 copy-start.6
  7.2 0.0 copy-start.7
  7.2 0.0 copy-start.2
  7.2 0.0 copy-start.4
  7.2 0.0 all-gather.2.cloned.1.call-start
  7.3 0.8 select_reduce_fusion
  8.1 0.2 copy-done
  8.3 0.7 gather_fusion
  8.9 0.0 copy-start.5
  9.0 0.1 broadcast_select_fusion
  9.1 24.4 %all_to_all.4 = bf16[8,64,576]{2,1,0:T(8,128)(2,1)} all-to-all(bf16[8,64,576]{2,1,0:T(8,128)(2,1)S(1)} %broadcast_select_fusion), channel_id=1, replica_groups=mesh['grp'=8,'head'=4] {'grp'}, dimensions={0} | all-to-all | bytes 1179648 | tf_op jit(solution)/shard_map/all_to_all | solution.py:33
  33.5 0.0 all-gather.2.cloned.1.call-update
  33.5 0.6 dynamic_slice.6
  36.1 0.0 copy-done.6
  36.1 0.6 dynamic_slice.7
  36.7 0.7 fusion.43
  37.3 0.0 copy-done.7
  37.3 0.1 iota_compare_fusion.1
  37.4 0.0 copy-done.2
  37.4 0.0 copy-done.4
  37.4 0.2 fusion.12
  37.6 0.2 fusion.55
  37.8 0.3 fusion.4
  38.1 34.2 %all-gather.2.cloned.1.call-done = bf16[2048,576]{1,0:T(8,128)(2,1)} async-done(((bf16[512,576]{1,0:T(8,128)(2,1)}), bf16[2048,576]{1,0:T(8,128)(2,1)}) %all-gather.2.cloned.1.call-update) | async-done | bytes 2359312 | tf_op jit(solution)/shard_map/all_gather | solution.py:53
  72.2 0.0 copy-done.5
  72.2 0.0 copy-start.1
  72.2 0.0 copy-start.3
  72.2 2.8 %fusion.54 = (f32[4]{0:T(128)S(1)}, f32[2048,4]{0,1:T(4,128)S(1)}) fusion(bf16[2048,576]{1,0:T(8,128)(2,1)} %all-gather.2.cloned.1.call-done, bf16[1,4,576]{2,1,0:T(4,128)(2,1)S(1)} %copy-done.5, pred[2048]{0:T(1024)(128)(4,1)S(1)} %fusion.43), kind=kOutput, calls=%fused_computation.72 | convolution fusion | flops 9461756 | bytes 2398736 | tf_op jit(solution)/shard_map/dot_general | solution.py:61
  75.0 0.2 fusion.22
  75.3 0.0 copy-done.1
  75.3 0.4 fusion.16
  75.7 0.0 copy-done.3
  75.7 2.7 %convolution_convert_fusion = bf16[5,3584]{1,0:T(8,128)(2,1)S(1)} fusion(bf16[512,3584]{1,0:T(8,128)(2,1)} %param.17, bf16[4,512,128]{2,1,0:T(8,128)(2,1)S(1)} %copy-done.3, bf16[5,4,512]{2,1,0:T(4,128)(2,1)S(1)} %pad_maximum_fusion), kind=kOutput, calls=%fused_computation.2 | convolution fusion | flops 20992000 | bytes 4250624 | tf_op jit(solution)/shard_map/dot_general | solution.py:83
  78.5 16.1 %psum.7 = bf16[5,3584]{1,0:T(8,128)(2,1)S(1)} all-reduce(bf16[5,3584]{1,0:T(8,128)(2,1)S(1)} %convolution_convert_fusion), channel_id=1, replica_groups=mesh['grp'=8,'head'=4] {'head'}, use_global_device_ids=true, to_apply=%region_5.6 | all-reduce | flops 17920 | bytes 71680 | tf_op jit(solution)/shard_map/psum | solution.py:84
  94.5 0.6 slice.19
  95.1 0.6 slice.20
  (5 shorter events, 0.1 us)
Async XLA Ops:
  7.2 1.1 %copy-start = (bf16[8,64,576]{2,1,0:T(8,128)(2,1)S(1)}, bf16[8,64,576]{2,1,0:T(8,128)(2,1)}, u32[]{:S(2)}) copy-start(bf16[8,64,576]{2,1,0:T(8,128)(2,1)} %param.12) | copy-start | bytes 1769476
  7.2 28.9 %copy-start.6 = (s32[8]{0:T(128)S(1)}, s32[8]{0:T(128)}, u32[]{:S(2)}) copy-start(s32[8]{0:T(128)} %param.13) | copy-start | bytes 100
  7.2 30.1 %copy-start.7 = (s32[4]{0:T(128)S(1)}, s32[4]{0:T(128)}, u32[]{:S(2)}) copy-start(s32[4]{0:T(128)} %param.10) | copy-start | bytes 52
  7.2 30.2 %copy-start.2 = (bf16[4,128,576]{1,2,0:T(8,128)(2,1)S(1)}, bf16[4,128,576]{1,2,0:T(8,128)(2,1)}, u32[]{:S(2)}) copy-start(bf16[4,128,576]{1,2,0:T(8,128)(2,1)} %param.9) | copy-start | bytes 1769476
  7.2 30.2 %copy-start.4 = (bf16[4,4,576]{2,1,0:T(4,128)(2,1)S(1)}, bf16[4,4,576]{2,1,0:T(4,128)(2,1)}, u32[]{:S(2)}) copy-start(bf16[4,4,576]{2,1,0:T(4,128)(2,1)} %param.11) | copy-start | bytes 55300
  7.2 65.0 %all-gather.2.cloned.1.call-start = ((), (), s32[]{:S(2)}) async-start(), calls=%async_computation.1 | async-start | bytes 3276800 | tf_op jit(solution)/shard_map/all_gather | solution.py:53
  8.9 63.3 %copy-start.5 = (bf16[1,4,576]{2,1,0:T(4,128)(2,1)S(1)}, bf16[1,4,576]{2,1,0:T(4,128)(2,1)}, u32[]{:S(2)}) copy-start(bf16[1,4,576]{2,1,0:T(4,128)(2,1)} %param.15) | copy-start | bytes 13828
  72.2 3.0 %copy-start.1 = (bf16[2048,576]{1,0:T(8,128)(2,1)S(1)}, bf16[2048,576]{1,0:T(8,128)(2,1)}, u32[]{:S(2)}) copy-start(bf16[2048,576]{1,0:T(8,128)(2,1)} %all-gather.2.cloned.1.call-done) | copy-start | bytes 7077892
  72.2 3.5 %copy-start.3 = (bf16[4,512,128]{2,1,0:T(8,128)(2,1)S(1)}, bf16[4,512,128]{2,1,0:T(8,128)(2,1)}, u32[]{:S(2)}) copy-start(bf16[4,512,128]{2,1,0:T(8,128)(2,1)} %param.16) | copy-start | bytes 1572868
Sparse Core Ops, SparseCore 0:
  33.6 38.5 all-gather.1
where the time goes:
time: 103 us
  blocking collectives  40.5 us (39%)
  waiting for transfers between devices  34.2 us (33%)
  between operations  16.1 us (16%)
  matrix products  6.43 us (6%)
  local copies, waits for them, and re-layouts  3.27 us (3%)
  other arithmetic  2.13 us (2%)
    all_gather x1, waiting for transfers between devices, per_device(): shard_rows = lax.all_gather(arrived, 'head', axis=0, tiled=True)  34.2 us
    all_to_all x1, blocking collectives, per_device(): lax.all_to_all(outgoing, 'grp', split_axis=0, concat_axis=1, tiled=True)[0]  24.4 us
    psum x1, blocking collectives, per_device(): mixed = lax.psum(partial_out.astype(jnp.bfloat16), 'head')  16.1 us
    dot_general x1, matrix products, per_device(): lax.dot_general(queries, shard_rows, (((1,), (1,)), ((), ())), preferred_...  2.78 us
    dot_general x1, matrix products, per_device(): partial_out = jnp.dot(head_rows, w_out, preferred_element_type=jnp.float32)  2.74 us
  transfers between devices with their start and end apart: 1, of which 1 were waited for; matrix products, arithmetic and copies ran while one was open for 2% of the time, Pallas kernels for 0%

commit v1 on v0

v1 whole, which is shorter than its diff:
```python
import functools

import jax
import jax.numpy as jnp
from jax import lax
from jax.experimental import pallas as pl
from jax.experimental.pallas import tpu as pltpu
from jax.sharding import PartitionSpec as P

score_scale = 192.0 ** (-0.5)
neg_large = -1e30
F32 = jnp.float32
BF16 = jnp.bfloat16
MESH = pl.DeviceIdType.MESH


def for_each(low, high, body):
    if high - low <= 4:
        for i in range(low, high):
            body(i)
    else:
        lax.fori_loop(low, high, lambda i, c: (body(i), c)[1], 0)


def attend(queries, tokens, mask, width):
    scores = (
        lax.dot_general(
            queries, tokens, (((1,), (1,)), ((), ())), preferred_element_type=F32
        )
        * score_scale
    )
    scores = jnp.where(mask, scores, neg_large)
    top = jnp.max(scores, axis=1, keepdims=True)
    top_hi = top.astype(BF16).astype(F32)
    rest = top - top_hi
    top_lo = (rest + jnp.abs(rest) * (2.0**-7)).astype(BF16).astype(F32)
    bound = top_hi + top_lo
    weights = jnp.where(mask, jnp.exp(scores - bound), 0.0)
    total = jnp.sum(weights, axis=1, keepdims=True)
    weighted = jnp.dot(
        weights.astype(BF16), tokens[:, :width], preferred_element_type=F32
    )
    return top_hi, top_lo, total, weighted


def up_project(latent, up_ref, heads):
    rows = latent.shape[0]
    head_of_row = lax.broadcasted_iota(jnp.int32, (rows, 1), 0) % heads
    out = None
    for head in range(heads):
        part = jnp.dot(latent, up_ref[head], preferred_element_type=F32)
        part = jnp.where(head_of_row == head, part, 0.0)
        out = part if out is None else out + part
    return out


def flatten_heads(values, heads):
    rows, width = values.shape
    head_of_row = lax.broadcasted_iota(jnp.int32, (rows, 1), 0) % heads
    wide = jnp.concatenate(
        [jnp.where(head_of_row == head, values, 0.0) for head in range(heads)], axis=1
    )
    return jnp.sum(wide.reshape(rows // heads, heads, heads * width), axis=1)


def kernel(
    n_grp,
    n_head,
    res_lengths,
    new_lengths,
    assignment,
    res_cache_hbm,
    res_query_hbm,
    new_cache_hbm,
    new_query_hbm,
    up_hbm,
    w_out_hbm,
    res_out,
    new_out,
    res_cache,
    res_query,
    new_cache,
    up,
    w_out,
    q_in,
    q_all,
    rep_out,
    rep_in,
    val_out,
    val_in,
    res_part,
    new_part,
    load_sem,
    r1_send,
    r1_recv,
    r2_send,
    r2_recv,
    r3_send,
    r3_recv,
    r4_send,
    r4_recv,
    r5_send,
    r5_recv,
    r6_send,
    r6_recv,
):
    grp = lax.axis_index("grp")
    head = lax.axis_index("head")
    residents, slots, latent = res_cache.shape
    heads = up.shape[0]
    width = up.shape[1]
    head_width = up.shape[2]
    requests, shard, _ = new_cache.shape
    features = w_out.shape[1]
    block_rows = n_grp * heads
    tokens = requests * shard
    splits = res_part.shape[1] // residents
    piece = features // splits

    loads = [
        pltpu.make_async_copy(src, dst, load_sem.at[i])
        for i, (src, dst) in enumerate(
            (
                (new_query_hbm.at[0], q_in.at[0]),
                (res_query_hbm, res_query),
                (res_cache_hbm, res_cache),
                (up_hbm, up),
                (new_cache_hbm, new_cache),
                (w_out_hbm, w_out),
            )
        )
    ]
    for load in loads:
        load.start()
    load_q, load_res_q, load_res, load_up, load_new, load_w = loads

    def grp_at(off):
        return lax.rem(grp + off, n_grp)

    def head_at(off):
        return lax.rem(head + off, n_head)

    barrier = pltpu.get_barrier_semaphore()

    def greet_grp(off):
        pl.semaphore_signal(
            barrier, inc=1, device_id=(grp_at(off), head), device_id_type=MESH
        )

    def greet_head(off):
        pl.semaphore_signal(
            barrier, inc=1, device_id=(grp, head_at(off)), device_id_type=MESH
        )

    for_each(1, n_grp, greet_grp)
    for_each(1, n_head, greet_head)

    def r1(off):
        return pltpu.make_async_remote_copy(
            src_ref=new_query_hbm.at[0],
            dst_ref=q_in.at[off],
            send_sem=r1_send.at[off],
            recv_sem=r1_recv.at[off],
            device_id=(grp_at(off), head),
            device_id_type=MESH,
        )

    def r2(off):
        return pltpu.make_async_remote_copy(
            src_ref=q_all.at[0],
            dst_ref=q_all.at[off],
            send_sem=r2_send.at[off],
            recv_sem=r2_recv.at[off],
            device_id=(grp, head_at(off)),
            device_id_type=MESH,
        )

    def r3(off):
        return pltpu.make_async_remote_copy(
            src_ref=rep_out.at[off],
            dst_ref=rep_in.at[off],
            send_sem=r3_send.at[off],
            recv_sem=r3_recv.at[off],
            device_id=(grp, head_at(n_head - off)),
            device_id_type=MESH,
        )

    def r4(off):
        return pltpu.make_async_remote_copy(
            src_ref=val_out.at[off],
            dst_ref=val_in.at[off],
            send_sem=r4_send.at[off],
            recv_sem=r4_recv.at[off],
            device_id=(grp_at(n_grp - off), head),
            device_id_type=MESH,
        )

    def r5(off):
        return pltpu.make_async_remote_copy(
            src_ref=res_part.at[head],
            dst_ref=res_part.at[head],
            send_sem=r5_send.at[off],
            recv_sem=r5_recv.at[off],
            device_id=(grp, head_at(off)),
            device_id_type=MESH,
        )

    def r6(off):
        return pltpu.make_async_remote_copy(
            src_ref=new_part.at[head],
            dst_ref=new_part.at[head],
            send_sem=r6_send.at[off],
            recv_sem=r6_recv.at[off],
            device_id=(grp, head_at(off)),
            device_id_type=MESH,
        )

    pl.semaphore_wait(barrier, n_grp - 1 + n_head - 1)
    for_each(1, n_grp, lambda off: r1(off).start())

    token = lax.broadcasted_iota(jnp.int32, (1, residents * slots), 1)
    row = lax.broadcasted_iota(jnp.int32, (residents * heads, 1), 0) // heads
    live = jnp.full((1, residents * slots), -1, jnp.int32)
    for r in range(residents):
        here = (token >= r * slots) & (token < r * slots + res_lengths[r])
        live = jnp.where(here, r, live)
    load_res_q.wait()
    load_res.wait()
    _, _, res_total, res_weighted = attend(
        res_query[...].astype(F32).reshape(residents * heads, latent).astype(BF16),
        res_cache[...].reshape(residents * slots, latent),
        row == live,
        width,
    )
    res_latent = (res_weighted / res_total).astype(BF16)
    load_up.wait()
    res_values = up_project(res_latent, up, heads).astype(BF16).astype(F32)
    res_rows = flatten_heads(res_values, heads).astype(BF16)

    first = (grp * n_head + head) * shard
    token = lax.broadcasted_iota(jnp.int32, (1, tokens), 1)
    asks = jnp.full((1, tokens), -1, jnp.int32)
    for k in range(requests):
        here = (token >= k * shard) & (token < k * shard + (new_lengths[k] - first))
        here = here & (token < (k + 1) * shard)
        asks = jnp.where(here, assignment[k], asks)
    row = lax.broadcasted_iota(jnp.int32, (block_rows, 1), 0) // heads
    group = grp - row
    group = jnp.where(group < 0, group + n_grp, group)
    mask = group == asks

    load_q.wait()
    for_each(1, n_grp, lambda off: r1(off).wait_recv())
    q_all[0] = q_in[...].astype(F32).reshape(block_rows, latent).astype(BF16)
    for_each(1, n_head, lambda off: r2(off).start())

    load_new.wait()

    def partials(off):
        return attend(
            q_all[off], new_cache[...].reshape(tokens, latent), mask, width
        )

    own_hi, own_lo, own_total, own_weighted = partials(0)

    lane = lax.broadcasted_iota(jnp.int32, (block_rows, 128), 1)

    def answer(off):
        r2(off).wait_recv()
        top_hi, top_lo, total, weighted = partials(off)
        total_hi = total.astype(BF16).astype(F32)
        stats = jnp.where(
            lane < 64,
            jnp.where(lane < 32, top_hi, top_lo),
            jnp.where(lane < 96, total_hi, total - total_hi),
        )
        rep_out[off] = jnp.concatenate([weighted, stats], axis=1).astype(BF16)
        r3(off).start()

    for_each(1, n_head, answer)

    load_w.wait()
    res_partial = jnp.dot(res_rows, w_out[...], preferred_element_type=F32)
    res_part[head] = jnp.concatenate(
        [res_partial[:, i * piece : (i + 1) * piece] for i in range(splits)], axis=0
    ).astype(BF16)
    for_each(1, n_head, lambda off: r5(off).start())

    for_each(1, n_head, lambda off: r3(off).wait_recv())
    tops = [own_hi + own_lo]
    totals = [own_total]
    for off in range(1, n_head):
        stats = rep_in[off, :, width:].astype(F32)
        tops.append(stats[:, 0:1] + stats[:, 32:33])
        totals.append(stats[:, 64:65] + stats[:, 96:97])
    top = functools.reduce(jnp.maximum, tops)
    share = jnp.exp(tops[0] - top)
    total = share * totals[0]
    summed = share * own_weighted
    for off in range(1, n_head):
        share = jnp.exp(tops[off] - top)
        total = total + share * totals[off]
        summed = summed + share * rep_in[off, :, :width].astype(F32)
    values = up_project(summed.astype(BF16), up, heads)
    lane = lax.broadcasted_iota(jnp.int32, (block_rows, 128), 1)
    stats = jnp.where(lane < 64, top, total)
    val_out[...] = jnp.concatenate([values, stats], axis=1).reshape(val_out.shape)
    for_each(1, n_grp, lambda off: r4(off).start())
    val_in[0] = val_out[0]

    for_each(1, n_head, lambda off: r5(off).wait_recv())
    res_sum = res_part[0].astype(F32)
    for rank in range(1, n_head):
        res_sum = res_sum + res_part[rank].astype(F32)
    for i in range(splits):
        res_out[:, i * piece : (i + 1) * piece] = res_sum[
            i * residents : (i + 1) * residents
        ].astype(BF16)

    for_each(1, n_grp, lambda off: r4(off).wait_recv())
    parts = val_in[...]
    tops = parts[:, :, head_width : head_width + 1]
    totals = parts[:, :, head_width + 64 : head_width + 65]
    top = jnp.max(tops, axis=0, keepdims=True)
    share = jnp.exp(tops - top)
    total = jnp.sum(share * totals, axis=0)
    values = jnp.sum(share * parts[:, :, :head_width], axis=0)
    values = (values / total).astype(BF16).astype(F32)
    new_row = flatten_heads(values, heads).astype(BF16)
    new_part[head] = jnp.dot(new_row, w_out[...], preferred_element_type=F32)
    for_each(1, n_head, lambda off: r6(off).start())
    for_each(1, n_head, lambda off: r6(off).wait_recv())
    new_sum = new_part[0]
    for rank in range(1, n_head):
        new_sum = new_sum + new_part[rank]
    new_out[...] = new_sum.astype(BF16)

    for_each(1, n_grp, lambda off: r1(off).wait_send())
    for_each(1, n_head, lambda off: r2(off).wait_send())
    for_each(1, n_head, lambda off: r3(off).wait_send())
    for_each(1, n_grp, lambda off: r4(off).wait_send())
    for_each(1, n_head, lambda off: r5(off).wait_send())
    for_each(1, n_head, lambda off: r6(off).wait_send())


def per_device(
    res_cache,
    res_lengths,
    res_query,
    new_cache,
    new_lengths,
    assignment,
    new_query,
    value_up_weight,
    w_out,
):
    n_grp = lax.axis_size("grp")
    n_head = lax.axis_size("head")
    residents = res_cache.shape[0]
    heads, width, head_width = value_up_weight.shape
    latent = res_cache.shape[2]
    features = w_out.shape[1]
    block_rows = n_grp * heads
    splits = 16 // residents
    smem = pl.BlockSpec(memory_space=pltpu.SMEM)
    anywhere = pl.BlockSpec(memory_space=pl.ANY)
    vmem = pl.BlockSpec(memory_space=pltpu.VMEM)
    dma = pltpu.SemaphoreType.DMA
    grp_sems = [dma((n_grp,)), dma((n_grp,))]
    head_sems = [dma((n_head,)), dma((n_head,))]
    return pl.pallas_call(
        functools.partial(kernel, n_grp, n_head),
        out_shape=(
            jax.ShapeDtypeStruct((residents, features), BF16),
            jax.ShapeDtypeStruct((1, features), BF16),
        ),
        in_specs=[smem] * 3 + [anywhere] * 6,
        out_specs=(vmem, vmem),
        scratch_shapes=[
            pltpu.VMEM(res_cache.shape, BF16),
            pltpu.VMEM(res_query.shape, BF16),
            pltpu.VMEM(new_cache.shape, BF16),
            pltpu.VMEM(value_up_weight.shape, BF16),
            pltpu.VMEM(w_out.shape, BF16),
            pltpu.VMEM((n_grp, heads, latent), BF16),
            pltpu.VMEM((n_head, block_rows, latent), BF16),
            pltpu.VMEM((n_head, block_rows, width + 128), BF16),
            pltpu.VMEM((n_head, block_rows, width + 128), BF16),
            pltpu.VMEM((n_grp, heads, head_width + 128), F32),
            pltpu.VMEM((n_grp, heads, head_width + 128), F32),
            pltpu.VMEM((n_head, residents * splits, features // splits), BF16),
            pltpu.VMEM((n_head, 1, features), F32),
            dma((6,)),
        ]
        + grp_sems
        + head_sems * 2
        + grp_sems
        + head_sems * 2,
        compiler_params=pltpu.CompilerParams(
            collective_id=0, has_side_effects=True, vmem_limit_bytes=48 * 2**20
        ),
    )(
        res_lengths,
        new_lengths,
        assignment,
        res_cache,
        res_query,
        new_cache,
        new_query,
        value_up_weight,
        w_out,
    )


def solution(mesh):
    in_specs = (
        P("grp", None, None),
        P("grp"),
        P("grp", "head", None),
        P(None, ("grp", "head"), None),
        P(),
        P(),
        P("grp", "head", None),
        P("head", None, None),
        P("head", None),
    )
    out_specs = (P("grp", None), P("grp", None))
    return jax.shard_map(
        per_device, mesh=mesh, in_specs=in_specs, out_specs=out_specs, check_vma=False
    )
```

time: 103 us -> 39.2 us (0.38)
  blocking collectives: 40.5 us -> 0 us
  waiting for transfers between devices: 34.2 us -> 0 us
  Pallas kernels: 0 us -> 28 us
  between operations: 16.1 us -> 0.66 us
  local copies, waits for them, and re-layouts: 3.27 us -> 10.1 us
  matrix products: 6.43 us -> 0 us
  other arithmetic: 2.13 us -> 0 us
    all_gather x1 -> x0, waiting for transfers between devices: 34.2 us -> none  [per_device(): shard_rows = lax.all_gather(arrived, 'head', axis=0, tiled=True)]
    pallas_call x0 -> x1, Pallas kernels: none -> 28 us  [per_device(): pl.pallas_call(functools.partial(kernel, n_grp, n_head), out_shape=(jax.S...]
    all_to_all x1 -> x0, blocking collectives: 24.4 us -> none  [per_device(): lax.all_to_all(outgoing, 'grp', split_axis=0, concat_axis=1, tiled=True)[0]]
    psum x1 -> x0, blocking collectives: 16.1 us -> none  [per_device(): mixed = lax.psum(partial_out.astype(jnp.bfloat16), 'head')]
    unnamed x16 -> x19, local copies, waits for them, and re-layouts: 0.2 us -> 10.1 us
    dot_general x5 -> x0, matrix products: 6.43 us -> none  [the longest x1 2.78 us: per_device(): lax.dot_general(queries, shard_rows, (((1,), (1,)), ((), ())), preferred_...]
    slice x2 -> x0, local copies, waits for them, and re-layouts: 1.24 us -> none  [per_device(): return (mixed[:resident], mixed[resident:])]
    dynamic_slice x2 -> x0, local copies, waits for them, and re-layouts: 1.17 us -> none  [per_device(): served_length = new_lengths[inverse[group_index]]]
  transfers between devices with their start and end apart: 1 -> 0, of which waited for: 1 -> 0; matrix products, arithmetic and copies ran while one was open for 2% -> 0% of each run, Pallas kernels for 0% -> 0%
where the time goes in v1:
time: 39.2 us; the launch traced here: 38.8 us
  Pallas kernels  28 us (71%)
  local copies, waits for them, and re-layouts  10.1 us (26%)
  between operations  0.66 us (2%)
    pallas_call x1, Pallas kernels, per_device(): pl.pallas_call(functools.partial(kernel, n_grp, n_head), out_shape=(jax.S...  28 us
    unnamed x19, local copies, waits for them, and re-layouts  10.1 us

profile of v1, /device:TPU:0, one launch (start us, length us, event | category | flops | bytes accessed | tf_op | source)
XLA Modules:
  0.0 38.8 jit_solution(17451582691943396066)
XLA Ops:
  0.6 1.4 %copy.11.res_cache_hbm = bf16[4,128,576]{2,1,0:T(8,128)(2,1)S(1)} copy(bf16[4,128,576]{1,2,0:T(8,128)(2,1)} %param.9) | data formatting | bytes 1179648 | tf_op args[0]
  2.0 0.0 copy-start
  2.0 2.0 %copy-done = bf16[512,3584]{1,0:T(8,128)(2,1)S(1)} copy-done((bf16[512,3584]{1,0:T(8,128)(2,1)S(1)}, bf16[512,3584]{1,0:T(8,128)(2,1)}, u32[]{:S(2)}) %copy-start) | copy-done | bytes 3670040
  4.0 0.0 copy-start.1
  4.0 1.1 %copy-done.1 = bf16[8,64,576]{2,1,0:T(8,128)(2,1)S(1)} copy-done((bf16[8,64,576]{2,1,0:T(8,128)(2,1)S(1)}, bf16[8,64,576]{2,1,0:T(8,128)(2,1)}, u32[]{:S(2)}) %copy-start.1) | copy-done | bytes 589848
  5.1 0.0 copy-start.2
  5.1 1.0 %copy-done.2 = bf16[4,512,128]{2,1,0:T(8,128)(2,1)S(1)} copy-done((bf16[4,512,128]{2,1,0:T(8,128)(2,1)S(1)}, bf16[4,512,128]{2,1,0:T(8,128)(2,1)}, u32[]{:S(2)}) %copy-start.2) | copy-done | bytes 524312
  6.2 0.0 copy-start.3
  6.2 0.7 %copy-done.3 = bf16[4,4,576]{2,1,0:T(4,128)(2,1)S(1)} copy-done((bf16[4,4,576]{2,1,0:T(4,128)(2,1)S(1)}, bf16[4,4,576]{2,1,0:T(4,128)(2,1)}, u32[]{:S(2)}) %copy-start.3) | copy-done | bytes 18456
  6.9 0.0 copy-start.4
  6.9 0.7 %copy-done.4 = bf16[1,4,576]{2,1,0:T(4,128)(2,1)S(1)} copy-done((bf16[1,4,576]{2,1,0:T(4,128)(2,1)S(1)}, bf16[1,4,576]{2,1,0:T(4,128)(2,1)}, u32[]{:S(2)}) %copy-start.4) | copy-done | bytes 4632
  7.6 0.0 copy-start.5
  7.6 0.7 %copy-done.5 = s32[4]{0:T(128)S(1)} copy-done((s32[4]{0:T(128)S(1)}, s32[4]{0:T(128)}, u32[]{:S(2)}) %copy-start.5) | copy-done | bytes 40
  8.2 0.0 copy-start.6
  8.2 0.7 %copy-done.6 = s32[8]{0:T(128)S(1)} copy-done((s32[8]{0:T(128)S(1)}, s32[8]{0:T(128)}, u32[]{:S(2)}) %copy-start.6) | copy-done | bytes 56
  8.9 0.0 copy-start.7
  8.9 0.7 %copy-done.7 = s32[8]{0:T(128)S(1)} copy-done((s32[8]{0:T(128)S(1)}, s32[8]{0:T(128)}, u32[]{:S(2)}) %copy-start.7) | copy-done | bytes 56
  9.5 28.0 %shard_map.104 = (bf16[4,3584]{1,0:T(4,128)(2,1)S(1)}, bf16[1,3584]{1,0:T(2,128)(2,1)S(1)}) custom-call(s32[4]{0:T(128)S(1)} %copy-done.5, s32[8]{0:T(128)S(1)} %copy-done.6, s32[8]{0:T(128)S(1)} %copy-done.7, bf16[4,128,576]{2,1,0:T(8,128)(2,1)S(1)} %copy.11.res_cache_hbm, bf16[4,4,576]{2,1,0:T(4,128)(2,1)S(1)} %copy-done.3, ...), custom_call_target="tpu_custom_call" | custom-call | tf_op jit(solution)/shard_map/pallas_call | solution.py:371
  37.6 0.6 %copy.14 = bf16[4,3584]{1,0:T(4,128)(2,1)} copy(bf16[4,3584]{1,0:T(4,128)(2,1)S(1)} %get-tuple-element.4) | data formatting | bytes 57344
  38.2 0.6 %copy.15 = bf16[1,3584]{1,0:T(2,128)(2,1)} copy(bf16[1,3584]{1,0:T(2,128)(2,1)S(1)} %get-tuple-element.5) | data formatting | bytes 14336
Async XLA Ops:
  2.0 2.0 %copy-start = (bf16[512,3584]{1,0:T(8,128)(2,1)S(1)}, bf16[512,3584]{1,0:T(8,128)(2,1)}, u32[]{:S(2)}) copy-start(bf16[512,3584]{1,0:T(8,128)(2,1)} %w_out_hbm.1) | copy-start | bytes 11010052
  4.0 1.1 %copy-start.1 = (bf16[8,64,576]{2,1,0:T(8,128)(2,1)S(1)}, bf16[8,64,576]{2,1,0:T(8,128)(2,1)}, u32[]{:S(2)}) copy-start(bf16[8,64,576]{2,1,0:T(8,128)(2,1)} %new_cache_hbm.1) | copy-start | bytes 1769476
  5.1 1.0 %copy-start.2 = (bf16[4,512,128]{2,1,0:T(8,128)(2,1)S(1)}, bf16[4,512,128]{2,1,0:T(8,128)(2,1)}, u32[]{:S(2)}) copy-start(bf16[4,512,128]{2,1,0:T(8,128)(2,1)} %up_hbm.1) | copy-start | bytes 1572868
  6.2 0.7 %copy-start.3 = (bf16[4,4,576]{2,1,0:T(4,128)(2,1)S(1)}, bf16[4,4,576]{2,1,0:T(4,128)(2,1)}, u32[]{:S(2)}) copy-start(bf16[4,4,576]{2,1,0:T(4,128)(2,1)} %res_query_hbm.1) | copy-start | bytes 55300
  6.9 0.7 %copy-start.4 = (bf16[1,4,576]{2,1,0:T(4,128)(2,1)S(1)}, bf16[1,4,576]{2,1,0:T(4,128)(2,1)}, u32[]{:S(2)}) copy-start(bf16[1,4,576]{2,1,0:T(4,128)(2,1)} %new_query_hbm.1) | copy-start | bytes 13828
  7.6 0.7 %copy-start.5 = (s32[4]{0:T(128)S(1)}, s32[4]{0:T(128)}, u32[]{:S(2)}) copy-start(s32[4]{0:T(128)} %res_lengths.1) | copy-start | bytes 52
  8.2 0.7 %copy-start.6 = (s32[8]{0:T(128)S(1)}, s32[8]{0:T(128)}, u32[]{:S(2)}) copy-start(s32[8]{0:T(128)} %new_lengths.1) | copy-start | bytes 100
  8.9 0.7 %copy-start.7 = (s32[8]{0:T(128)S(1)}, s32[8]{0:T(128)}, u32[]{:S(2)}) copy-start(s32[8]{0:T(128)} %assignment.1) | copy-start | bytes 100

commit v2 on v1

--- a/solution.py
+++ b/solution.py
@@ -29,6 +29,12 @@
         )
         * score_scale
     )
+    top_hi, top_lo, total, weights = soften(scores, mask)
+    weighted = jnp.dot(weights, tokens[:, :width], preferred_element_type=F32)
+    return top_hi, top_lo, total, weighted
+
+
+def soften(scores, mask):
     scores = jnp.where(mask, scores, neg_large)
     top = jnp.max(scores, axis=1, keepdims=True)
     top_hi = top.astype(BF16).astype(F32)
@@ -37,10 +43,7 @@
     bound = top_hi + top_lo
     weights = jnp.where(mask, jnp.exp(scores - bound), 0.0)
     total = jnp.sum(weights, axis=1, keepdims=True)
-    weighted = jnp.dot(
-        weights.astype(BF16), tokens[:, :width], preferred_element_type=F32
-    )
-    return top_hi, top_lo, total, weighted
+    return top_hi, top_lo, total, weights.astype(BF16)
 
 
 def up_project(latent, up_ref, heads):
@@ -66,9 +69,9 @@
 def kernel(
     n_grp,
     n_head,
-    res_lengths,
-    new_lengths,
-    assignment,
+    res_lengths_hbm,
+    new_lengths_hbm,
+    assignment_hbm,
     res_cache_hbm,
     res_query_hbm,
     new_cache_hbm,
@@ -77,6 +80,9 @@
     w_out_hbm,
     res_out,
     new_out,
+    res_lengths,
+    new_lengths,
+    assignment,
     res_cache,
     res_query,
     new_cache,
@@ -106,7 +112,7 @@
 ):
     grp = lax.axis_index("grp")
     head = lax.axis_index("head")
-    residents, slots, latent = res_cache.shape
+    residents, latent, slots = res_cache.shape
     heads = up.shape[0]
     width = up.shape[1]
     head_width = up.shape[2]
@@ -122,6 +128,9 @@
         for i, (src, dst) in enumerate(
             (
                 (new_query_hbm.at[0], q_in.at[0]),
+                (res_lengths_hbm, res_lengths),
+                (new_lengths_hbm, new_lengths),
+                (assignment_hbm, assignment),
                 (res_query_hbm, res_query),
                 (res_cache_hbm, res_cache),
                 (up_hbm, up),
@@ -132,7 +141,7 @@
     ]
     for load in loads:
         load.start()
-    load_q, load_res_q, load_res, load_up, load_new, load_w = loads
+    load_q, load_l, load_n, load_a, load_res_q, load_res, load_up, load_new, load_w = loads
 
     def grp_at(off):
         return lax.rem(grp + off, n_grp)
@@ -221,17 +230,27 @@
     token = lax.broadcasted_iota(jnp.int32, (1, residents * slots), 1)
     row = lax.broadcasted_iota(jnp.int32, (residents * heads, 1), 0) // heads
     live = jnp.full((1, residents * slots), -1, jnp.int32)
+    load_l.wait()
     for r in range(residents):
         here = (token >= r * slots) & (token < r * slots + res_lengths[r])
         live = jnp.where(here, r, live)
     load_res_q.wait()
     load_res.wait()
-    _, _, res_total, res_weighted = attend(
-        res_query[...].astype(F32).reshape(residents * heads, latent).astype(BF16),
-        res_cache[...].reshape(residents * slots, latent),
-        row == live,
-        width,
-    )
+    queries = res_query[...].astype(F32).reshape(residents * heads, latent).astype(BF16)
+    scores = [
+        jnp.dot(queries, res_cache[r], preferred_element_type=F32) * score_scale
+        for r in range(residents)
+    ]
+    _, _, res_total, weights = soften(jnp.concatenate(scores, axis=1), row == live)
+    res_weighted = None
+    for r in range(residents):
+        part = lax.dot_general(
+            weights[:, r * slots : (r + 1) * slots],
+            res_cache[r, :width, :],
+            (((1,), (1,)), ((), ())),
+            preferred_element_type=F32,
+        )
+        res_weighted = part if res_weighted is None else res_weighted + part
     res_latent = (res_weighted / res_total).astype(BF16)
     load_up.wait()
     res_values = up_project(res_latent, up, heads).astype(BF16).astype(F32)
@@ -240,6 +259,8 @@
     first = (grp * n_head + head) * shard
     token = lax.broadcasted_iota(jnp.int32, (1, tokens), 1)
     asks = jnp.full((1, tokens), -1, jnp.int32)
+    load_n.wait()
+    load_a.wait()
     for k in range(requests):
         here = (token >= k * shard) & (token < k * shard + (new_lengths[k] - first))
         here = here & (token < (k + 1) * shard)
@@ -256,28 +277,43 @@
 
     load_new.wait()
 
-    def partials(off):
-        return attend(
-            q_all[off], new_cache[...].reshape(tokens, latent), mask, width
-        )
-
-    own_hi, own_lo, own_total, own_weighted = partials(0)
-
-    lane = lax.broadcasted_iota(jnp.int32, (block_rows, 128), 1)
-
-    def answer(off):
-        r2(off).wait_recv()
-        top_hi, top_lo, total, weighted = partials(off)
+    own_hi, own_lo, own_total, own_weighted = attend(
+        q_all[0], new_cache[...].reshape(tokens, latent), mask, width
+    )
+
+    def answer(low, count):
+        rows = count * block_rows
+        top_hi, top_lo, total, weighted = attend(
+            q_all[pl.ds(low, count)].reshape(rows, latent),
+            new_cache[...].reshape(tokens, latent),
+            jnp.concatenate([mask] * count, axis=0),
+            width,
+        )
         total_hi = total.astype(BF16).astype(F32)
+        lane = lax.broadcasted_iota(jnp.int32, (rows, 128), 1)
         stats = jnp.where(
             lane < 64,
             jnp.where(lane < 32, top_hi, top_lo),
             jnp.where(lane < 96, total_hi, total - total_hi),
         )
-        rep_out[off] = jnp.concatenate([weighted, stats], axis=1).astype(BF16)
-        r3(off).start()
-
-    for_each(1, n_head, answer)
+        rep_out[pl.ds(low, count)] = (
+            jnp.concatenate([weighted, stats], axis=1)
+            .astype(BF16)
+            .reshape(count, block_rows, width + 128)
+        )
+
+    if (n_head - 1) * block_rows <= 128:
+        for_each(1, n_head, lambda off: r2(off).wait_recv())
+        answer(1, n_head - 1)
+        for_each(1, n_head, lambda off: r3(off).start())
+    else:
+
+        def answer_one(off):
+            r2(off).wait_recv()
+            answer(off, 1)
+            r3(off).start()
+
+        for_each(1, n_head, answer_one)
 
     load_w.wait()
     res_partial = jnp.dot(res_rows, w_out[...], preferred_element_type=F32)
@@ -359,11 +395,11 @@
     residents = res_cache.shape[0]
     heads, width, head_width = value_up_weight.shape
     latent = res_cache.shape[2]
+    res_cache = jnp.swapaxes(res_cache, 1, 2)
     features = w_out.shape[1]
     block_rows = n_grp * heads
     splits = 16 // residents
-    smem = pl.BlockSpec(memory_space=pltpu.SMEM)
-    anywhere = pl.BlockSpec(memory_space=pl.ANY)
+    hbm = pl.BlockSpec(memory_space=pltpu.HBM)
     vmem = pl.BlockSpec(memory_space=pltpu.VMEM)
     dma = pltpu.SemaphoreType.DMA
     grp_sems = [dma((n_grp,)), dma((n_grp,))]
@@ -374,9 +410,12 @@
             jax.ShapeDtypeStruct((residents, features), BF16),
             jax.ShapeDtypeStruct((1, features), BF16),
         ),
-        in_specs=[smem] * 3 + [anywhere] * 6,
+        in_specs=[hbm] * 9,
         out_specs=(vmem, vmem),
         scratch_shapes=[
+            pltpu.SMEM(res_lengths.shape, jnp.int32),
+            pltpu.SMEM(new_lengths.shape, jnp.int32),
+            pltpu.SMEM(assignment.shape, jnp.int32),
             pltpu.VMEM(res_cache.shape, BF16),
             pltpu.VMEM(res_query.shape, BF16),
             pltpu.VMEM(new_cache.shape, BF16),
@@ -390,14 +429,14 @@
             pltpu.VMEM((n_grp, heads, head_width + 128), F32),
             pltpu.VMEM((n_head, residents * splits, features // splits), BF16),
             pltpu.VMEM((n_head, 1, features), F32),
-            dma((6,)),
+            dma((9,)),
         ]
         + grp_sems
         + head_sems * 2
         + grp_sems
         + head_sems * 2,
         compiler_params=pltpu.CompilerParams(
-            collective_id=0, has_side_effects=True, vmem_limit_bytes=48 * 2**20
+            collective_id=0, has_side_effects=True, vmem_limit_bytes=60 * 2**20
         ),
     )(
         res_lengths,

time: 39.2 us -> 31.1 us (0.79)
  local copies, waits for them, and re-layouts: 10.1 us -> 2.69 us
  Pallas kernels: 28 us -> 27.5 us
    unnamed x19 -> x2, local copies, waits for them, and re-layouts: 10.1 us -> 2.69 us
    pallas_call x1, Pallas kernels: 28 us -> 27.5 us  [per_device(): pl.pallas_call(functools.partial(kernel, n_grp, n_head), out_shape=(jax.S...]
where the time goes in v2:
time: 31.1 us; the launch traced here: 30.9 us
  Pallas kernels  27.5 us (88%)
  local copies, waits for them, and re-layouts  2.69 us (9%)
  between operations  0.64 us (2%)
    pallas_call x1, Pallas kernels, per_device(): pl.pallas_call(functools.partial(kernel, n_grp, n_head), out_shape=(jax.S...  27.5 us
    unnamed x2, local copies, waits for them, and re-layouts  2.69 us

profile of v2, /device:TPU:0, one launch (start us, length us, event | category | flops | bytes accessed | tf_op | source)
XLA Modules:
  0.0 30.9 jit_solution(3086138757076862364)
XLA Ops:
  0.6 27.5 %shard_map.104 = (bf16[4,3584]{1,0:T(4,128)(2,1)}, bf16[1,3584]{1,0:T(2,128)(2,1)}) custom-call(s32[4]{0:T(128)} %res_lengths_hbm.1, s32[8]{0:T(128)} %new_lengths_hbm.1, s32[8]{0:T(128)} %assignment_hbm.1, bf16[4,576,128]{2,1,0:T(8,128)(2,1)} %bitcast.1, bf16[4,4,576]{2,1,0:T(4,128)(2,1)} %res_query_hbm.1, bf16[8,64,576]{2,1,0:T(8,128)(2,1)} %new_cache_hbm.1, ...), custom_call_target="tpu_custom_call" | custom-call | tf_op jit(solution)/shard_map/pallas_call | solution.py:407
  28.2 1.4 %copy.13 = bf16[4,3584]{1,0:T(4,128)(2,1)} copy(bf16[4,3584]{1,0:T(4,128)(2,1)} %get-tuple-element.4) | data formatting | bytes 57344
  29.5 1.3 %copy.14 = bf16[1,3584]{1,0:T(2,128)(2,1)} copy(bf16[1,3584]{1,0:T(2,128)(2,1)} %get-tuple-element.5) | data formatting | bytes 14336

commit v3 on v2

v3 whole, which is shorter than its diff:
```python
import functools

import jax
import jax.numpy as jnp
from jax import lax
from jax.experimental import pallas as pl
from jax.experimental.pallas import tpu as pltpu
from jax.sharding import PartitionSpec as P

score_scale = 192.0 ** (-0.5)
neg_large = -1e30
F32 = jnp.float32
BF16 = jnp.bfloat16
MESH = pl.DeviceIdType.MESH


def for_each(low, high, body):
    if high - low < 32:
        for i in range(low, high):
            body(i)
    else:
        lax.fori_loop(low, high, lambda i, c: (body(i), c)[1], 0)


def attend(queries, tokens, mask, width):
    scores = (
        lax.dot_general(
            queries, tokens, (((1,), (1,)), ((), ())), preferred_element_type=F32
        )
        * score_scale
    )
    top_hi, top_lo, total, weights = soften(scores, mask)
    weighted = jnp.dot(weights, tokens[:, :width], preferred_element_type=F32)
    return top_hi, top_lo, total, weighted


def soften(scores, mask):
    scores = jnp.where(mask, scores, neg_large)
    top = jnp.max(scores, axis=1, keepdims=True)
    top_hi = top.astype(BF16).astype(F32)
    rest = top - top_hi
    top_lo = (rest + jnp.abs(rest) * (2.0**-7)).astype(BF16).astype(F32)
    bound = top_hi + top_lo
    weights = jnp.where(mask, jnp.exp(scores - bound), 0.0)
    total = jnp.sum(weights, axis=1, keepdims=True)
    return top_hi, top_lo, total, weights.astype(BF16)


def up_project(latent, up_ref, heads):
    rows = latent.shape[0]
    head_of_row = lax.broadcasted_iota(jnp.int32, (rows, 1), 0) % heads
    out = None
    for head in range(heads):
        part = jnp.dot(latent, up_ref[head], preferred_element_type=F32)
        part = jnp.where(head_of_row == head, part, 0.0)
        out = part if out is None else out + part
    return out


def flatten_heads(values, heads):
    rows, width = values.shape
    head_of_row = lax.broadcasted_iota(jnp.int32, (rows, 1), 0) % heads
    wide = jnp.concatenate(
        [jnp.where(head_of_row == head, values, 0.0) for head in range(heads)], axis=1
    )
    return jnp.sum(wide.reshape(rows // heads, heads, heads * width), axis=1)


def kernel(
    n_grp,
    n_head,
    res_lengths_hbm,
    new_lengths_hbm,
    assignment_hbm,
    res_cache_hbm,
    res_query_hbm,
    new_cache_hbm,
    new_query_hbm,
    up_hbm,
    w_out_hbm,
    res_out,
    new_out,
    res_lengths,
    new_lengths,
    assignment,
    res_cache,
    res_query,
    new_cache,
    up,
    w_out,
    q_in,
    rep_out,
    rep_in,
    res_part,
    new_part,
    load_sem,
    ask_send,
    ask_recv,
    answer_send,
    answer_recv,
    res_send,
    res_recv,
    new_send,
    new_recv,
):
    grp = lax.axis_index("grp")
    head = lax.axis_index("head")
    residents, latent, slots = res_cache.shape
    heads, width, head_width = up.shape
    requests, shard, _ = new_cache.shape
    features = w_out.shape[1]
    devices = n_grp * n_head
    tokens = requests * shard
    splits = res_part.shape[1] // residents
    piece = features // splits
    chunk = min(devices, 32)
    rows = chunk * heads

    loads = [
        pltpu.make_async_copy(src, dst, load_sem.at[i])
        for i, (src, dst) in enumerate(
            (
                (new_query_hbm.at[0], q_in.at[0]),
                (res_lengths_hbm, res_lengths),
                (new_lengths_hbm, new_lengths),
                (assignment_hbm, assignment),
                (res_query_hbm, res_query),
                (res_cache_hbm, res_cache),
                (up_hbm, up),
                (new_cache_hbm, new_cache),
                (w_out_hbm, w_out),
            )
        )
    ]
    load_q, load_l, load_n, load_a, load_res_q, load_res, load_up, load_new, load_w = loads

    def ahead(slot):
        return (
            lax.rem(grp + slot // n_head, n_grp),
            lax.rem(head + slot % n_head, n_head),
        )

    def behind(slot):
        return (
            lax.rem(grp + n_grp - slot // n_head, n_grp),
            lax.rem(head + n_head - slot % n_head, n_head),
        )

    def head_at(off):
        return (grp, lax.rem(head + off, n_head))

    barrier = pltpu.get_barrier_semaphore()

    def greet(slot):
        pl.semaphore_signal(
            barrier, inc=1, device_id=ahead(slot), device_id_type=MESH
        )

    for_each(1, devices, greet)
    for load in loads:
        load.start()

    def ask(slot):
        return pltpu.make_async_remote_copy(
            src_ref=new_query_hbm.at[0],
            dst_ref=q_in.at[slot],
            send_sem=ask_send.at[slot],
            recv_sem=ask_recv.at[slot],
            device_id=ahead(slot),
            device_id_type=MESH,
        )

    def answer(slot):
        return pltpu.make_async_remote_copy(
            src_ref=rep_out.at[slot],
            dst_ref=rep_in.at[slot],
            send_sem=answer_send.at[slot],
            recv_sem=answer_recv.at[slot],
            device_id=behind(slot),
            device_id_type=MESH,
        )

    def share_res(off):
        return pltpu.make_async_remote_copy(
            src_ref=res_part.at[head],
            dst_ref=res_part.at[head],
            send_sem=res_send.at[off],
            recv_sem=res_recv.at[off],
            device_id=head_at(off),
            device_id_type=MESH,
        )

    def share_new(off):
        return pltpu.make_async_remote_copy(
            src_ref=new_part.at[head],
            dst_ref=new_part.at[head],
            send_sem=new_send.at[off],
            recv_sem=new_recv.at[off],
            device_id=head_at(off),
            device_id_type=MESH,
        )

    pl.semaphore_wait(barrier, devices - 1)
    for_each(1, devices, lambda slot: ask(slot).start())

    token = lax.broadcasted_iota(jnp.int32, (1, residents * slots), 1)
    row = lax.broadcasted_iota(jnp.int32, (residents * heads, 1), 0) // heads
    live = jnp.full((1, residents * slots), -1, jnp.int32)
    load_l.wait()
    for r in range(residents):
        here = (token >= r * slots) & (token < r * slots + res_lengths[r])
        live = jnp.where(here, r, live)
    load_res_q.wait()
    load_res.wait()
    queries = res_query[...].astype(F32).reshape(residents * heads, latent).astype(BF16)
    scores = [
        jnp.dot(queries, res_cache[r], preferred_element_type=F32) * score_scale
        for r in range(residents)
    ]
    _, _, res_total, weights = soften(jnp.concatenate(scores, axis=1), row == live)
    res_weighted = None
    for r in range(residents):
        part = lax.dot_general(
            weights[:, r * slots : (r + 1) * slots],
            res_cache[r, :width, :],
            (((1,), (1,)), ((), ())),
            preferred_element_type=F32,
        )
        res_weighted = part if res_weighted is None else res_weighted + part
    res_latent = (res_weighted / res_total).astype(BF16)
    load_up.wait()
    res_values = up_project(res_latent, up, heads).astype(BF16).astype(F32)
    res_rows = flatten_heads(res_values, heads).astype(BF16)
    load_w.wait()
    res_partial = jnp.dot(res_rows, w_out[...], preferred_element_type=F32)
    res_part[head] = jnp.concatenate(
        [res_partial[:, i * piece : (i + 1) * piece] for i in range(splits)], axis=0
    ).astype(BF16)

    first = (grp * n_head + head) * shard
    token = lax.broadcasted_iota(jnp.int32, (1, tokens), 1)
    asks = jnp.full((1, tokens), -1, jnp.int32)
    load_n.wait()
    load_a.wait()
    for k in range(requests):
        here = (token >= k * shard) & (token < k * shard + (new_lengths[k] - first))
        here = here & (token < (k + 1) * shard)
        asks = jnp.where(here, assignment[k], asks)
    row = lax.broadcasted_iota(jnp.int32, (rows, 1), 0) // (heads * n_head)
    lane = lax.broadcasted_iota(jnp.int32, (rows, 128), 1)
    load_new.wait()
    load_q.wait()

    def attend_chunk(low):
        group = grp - row - low // n_head
        group = jnp.where(group < 0, group + n_grp, group)
        top_hi, top_lo, total, weighted = attend(
            q_in[pl.ds(low, chunk)].astype(F32).reshape(rows, latent).astype(BF16),
            new_cache[...].reshape(tokens, latent),
            group == asks,
            width,
        )
        total_hi = total.astype(BF16).astype(F32)
        stats = jnp.where(
            lane < 64,
            jnp.where(lane < 32, top_hi, top_lo),
            jnp.where(lane < 96, total_hi, total - total_hi),
        )
        rep_out[pl.ds(low, chunk)] = (
            jnp.concatenate([weighted, stats], axis=1)
            .reshape(chunk, heads, width + 128)
            .astype(BF16)
        )

    for_each(1, devices, lambda slot: ask(slot).wait_recv())
    for_each(0, devices // chunk, lambda i: attend_chunk(i * chunk))
    for_each(1, devices, lambda slot: answer(slot).start())
    for_each(1, n_head, lambda off: share_res(off).start())
    rep_in[0] = rep_out[0]
    for_each(1, devices, lambda slot: ask(slot).wait_send())

    def add_chunk(low, so_far):
        parts = rep_in[pl.ds(low, chunk)].astype(F32)
        tops = parts[:, :, width : width + 1] + parts[:, :, width + 32 : width + 33]
        totals = (
            parts[:, :, width + 64 : width + 65] + parts[:, :, width + 96 : width + 97]
        )
        top = jnp.max(tops, axis=0)
        if so_far is not None:
            top = jnp.maximum(top, so_far[0])
        share = jnp.exp(tops - top[None])
        total = jnp.sum(share * totals, axis=0)
        summed = jnp.sum(share * parts[:, :, :width], axis=0)
        if so_far is not None:
            share = jnp.exp(so_far[0] - top)
            total = total + share * so_far[1]
            summed = summed + share * so_far[2]
        return top, total, summed

    for_each(1, devices, lambda slot: answer(slot).wait_recv())
    sums = add_chunk(0, None)
    if devices > chunk:
        sums = lax.fori_loop(
            1, devices // chunk, lambda i, so_far: add_chunk(i * chunk, so_far), sums
        )
    _, total, summed = sums
    new_latent = (summed / total).astype(BF16)
    new_values = up_project(new_latent, up, heads).astype(BF16).astype(F32)
    new_row = flatten_heads(new_values, heads).astype(BF16)
    new_part[head] = jnp.dot(new_row, w_out[...], preferred_element_type=F32)
    for_each(1, n_head, lambda off: share_new(off).start())

    for_each(1, devices, lambda slot: answer(slot).wait_send())
    for_each(1, n_head, lambda off: share_res(off).wait_recv())
    res_sum = res_part[0].astype(F32)
    for rank in range(1, n_head):
        res_sum = res_sum + res_part[rank].astype(F32)
    for i in range(splits):
        res_out[:, i * piece : (i + 1) * piece] = res_sum[
            i * residents : (i + 1) * residents
        ].astype(BF16)
    for_each(1, n_head, lambda off: share_res(off).wait_send())
    for_each(1, n_head, lambda off: share_new(off).wait_recv())
    new_sum = new_part[0]
    for rank in range(1, n_head):
        new_sum = new_sum + new_part[rank]
    new_out[...] = new_sum.astype(BF16)
    for_each(1, n_head, lambda off: share_new(off).wait_send())


def write_back(res_in, new_in, res_out, new_out, sem):
    copies = [
        pltpu.make_async_copy(res_in, res_out, sem.at[0]),
        pltpu.make_async_copy(new_in, new_out, sem.at[1]),
    ]
    for copy in copies:
        copy.start()
    for copy in copies:
        copy.wait()


def per_device(
    res_cache,
    res_lengths,
    res_query,
    new_cache,
    new_lengths,
    assignment,
    new_query,
    value_up_weight,
    w_out,
):
    n_grp = lax.axis_size("grp")
    n_head = lax.axis_size("head")
    devices = n_grp * n_head
    residents = res_cache.shape[0]
    heads, width, head_width = value_up_weight.shape
    latent = res_cache.shape[2]
    res_cache = jnp.swapaxes(res_cache, 1, 2)
    features = w_out.shape[1]
    splits = 16 // residents
    hbm = pl.BlockSpec(memory_space=pltpu.HBM)
    vmem = pl.BlockSpec(memory_space=pltpu.VMEM)
    dma = pltpu.SemaphoreType.DMA
    results = pl.pallas_call(
        functools.partial(kernel, n_grp, n_head),
        out_shape=(
            pltpu.VMEM((residents, features), BF16),
            pltpu.VMEM((1, features), BF16),
        ),
        in_specs=[hbm] * 9,
        out_specs=(vmem, vmem),
        scratch_shapes=[
            pltpu.SMEM(res_lengths.shape, jnp.int32),
            pltpu.SMEM(new_lengths.shape, jnp.int32),
            pltpu.SMEM(assignment.shape, jnp.int32),
            pltpu.VMEM(res_cache.shape, BF16),
            pltpu.VMEM(res_query.shape, BF16),
            pltpu.VMEM(new_cache.shape, BF16),
            pltpu.VMEM(value_up_weight.shape, BF16),
            pltpu.VMEM(w_out.shape, BF16),
            pltpu.VMEM((devices, heads, latent), BF16),
            pltpu.VMEM((devices, heads, width + 128), BF16),
            pltpu.VMEM((devices, heads, width + 128), BF16),
            pltpu.VMEM((n_head, residents * splits, features // splits), BF16),
            pltpu.VMEM((n_head, 1, features), F32),
            dma((9,)),
        ]
        + [dma((devices,))] * 4
        + [dma((n_head,))] * 4,
        compiler_params=pltpu.CompilerParams(
            collective_id=0, has_side_effects=True, vmem_limit_bytes=60 * 2**20
        ),
    )(
        res_lengths,
        new_lengths,
        assignment,
        res_cache,
        res_query,
        new_cache,
        new_query,
        value_up_weight,
        w_out,
    )
    return pl.pallas_call(
        write_back,
        out_shape=tuple(jax.ShapeDtypeStruct(r.shape, r.dtype) for r in results),
        in_specs=[vmem, vmem],
        out_specs=(hbm, hbm),
        scratch_shapes=[dma((2,))],
    )(*results)


def solution(mesh):
    in_specs = (
        P("grp", None, None),
        P("grp"),
        P("grp", "head", None),
        P(None, ("grp", "head"), None),
        P(),
        P(),
        P("grp", "head", None),
        P("head", None, None),
        P("head", None),
    )
    out_specs = (P("grp", None), P("grp", None))
    return jax.shard_map(
        per_device, mesh=mesh, in_specs=in_specs, out_specs=out_specs, check_vma=False
    )
```

time: 31.1 us -> 28.9 us (0.929)
  local copies, waits for them, and re-layouts: 2.69 us -> 1.2 us
  Pallas kernels: 27.5 us -> 26.8 us
    unnamed x2 -> x4, local copies, waits for them, and re-layouts: 2.69 us -> 1.2 us
    pallas_call x1 -> x2, Pallas kernels: 27.5 us -> 26.8 us  [the longest x1 25.5 us: per_device(): pl.pallas_call(functools.partial(kernel, n_grp, n_head), out_shape=(pltpu...]
where the time goes in v3:
time: 28.9 us; the launch traced here: 28.7 us
  Pallas kernels  26.8 us (93%)
  local copies, waits for them, and re-layouts  1.2 us (4%)
  between operations  0.65 us (2%)
    pallas_call x1, Pallas kernels, per_device(): pl.pallas_call(functools.partial(kernel, n_grp, n_head), out_shape=(pltpu...  25.5 us
    pallas_call x1, Pallas kernels, per_device(): pl.pallas_call(write_back, out_shape=tuple((jax.ShapeDtypeStruct(r.shape,...  1.38 us
    unnamed x4, local copies, waits for them, and re-layouts  1.2 us

profile of v3, /device:TPU:0, one launch (start us, length us, event | category | flops | bytes accessed | tf_op | source)
XLA Modules:
  0.0 28.7 jit_solution(10076973232900924467)
XLA Ops:
  0.6 25.5 %shard_map.104 = (bf16[4,3584]{1,0:T(4,128)(2,1)S(1)}, bf16[1,3584]{1,0:T(2,128)(2,1)S(1)}) custom-call(s32[4]{0:T(128)} %res_lengths_hbm.1, s32[8]{0:T(128)} %new_lengths_hbm.1, s32[8]{0:T(128)} %assignment_hbm.1, bf16[4,576,128]{2,1,0:T(8,128)(2,1)} %bitcast.1, bf16[4,4,576]{2,1,0:T(4,128)(2,1)} %res_query_hbm.1, bf16[8,64,576]{2,1,0:T(8,128)(2,1)} %new_cache_hbm.1, ...), custom_call_target="tpu_custom_call" | custom-call | tf_op jit(solution)/shard_map/pallas_call | solution.py:365
  26.1 0.0 copy-start
  26.1 0.6 %copy-done = bf16[4,3584]{1,0:T(4,128)(2,1)} copy-done((bf16[4,3584]{1,0:T(4,128)(2,1)}, bf16[4,3584]{1,0:T(4,128)(2,1)S(1)}, u32[]{:S(2)}) %copy-start) | copy-done | bytes 28696
  26.7 0.0 copy-start.1
  26.7 0.6 %copy-done.1 = bf16[1,3584]{1,0:T(2,128)(2,1)} copy-done((bf16[1,3584]{1,0:T(2,128)(2,1)}, bf16[1,3584]{1,0:T(2,128)(2,1)S(1)}, u32[]{:S(2)}) %copy-start.1) | copy-done | bytes 7192
  27.3 1.4 %shard_map.105 = (bf16[4,3584]{1,0:T(4,128)(2,1)}, bf16[1,3584]{1,0:T(2,128)(2,1)}) custom-call(bf16[4,3584]{1,0:T(4,128)(2,1)} %copy-done, bf16[1,3584]{1,0:T(2,128)(2,1)} %copy-done.1), custom_call_target="tpu_custom_call" | custom-call | tf_op jit(solution)/shard_map/pallas_call | solution.py:405
Async XLA Ops:
  26.1 0.6 %copy-start = (bf16[4,3584]{1,0:T(4,128)(2,1)}, bf16[4,3584]{1,0:T(4,128)(2,1)S(1)}, u32[]{:S(2)}) copy-start(bf16[4,3584]{1,0:T(4,128)(2,1)S(1)} %get-tuple-element.4.res_in) | copy-start | bytes 86020
  26.7 0.6 %copy-start.1 = (bf16[1,3584]{1,0:T(2,128)(2,1)}, bf16[1,3584]{1,0:T(2,128)(2,1)S(1)}, u32[]{:S(2)}) copy-start(bf16[1,3584]{1,0:T(2,128)(2,1)S(1)} %get-tuple-element.5.new_in) | copy-start | bytes 21508

commit v4 on v3

--- a/solution.py
+++ b/solution.py
@@ -94,6 +94,7 @@
     res_part,
     new_part,
     load_sem,
+    swap_sem,
     ask_send,
     ask_recv,
     answer_send,
@@ -107,13 +108,14 @@
     head = lax.axis_index("head")
     residents, latent, slots = res_cache.shape
     heads, width, head_width = up.shape
-    requests, shard, _ = new_cache.shape
+    _, requests, shard, _ = new_cache.shape
     features = w_out.shape[1]
-    devices = n_grp * n_head
-    tokens = requests * shard
+    peers = n_grp // 2 * n_head
+    sibling = grp + 1 - 2 * lax.rem(grp, 2)
+    tokens = 2 * requests * shard
     splits = res_part.shape[1] // residents
     piece = features // splits
-    chunk = min(devices, 32)
+    chunk = min(peers, 16)
     rows = chunk * heads
 
     loads = [
@@ -127,7 +129,7 @@
                 (res_query_hbm, res_query),
                 (res_cache_hbm, res_cache),
                 (up_hbm, up),
-                (new_cache_hbm, new_cache),
+                (new_cache_hbm, new_cache.at[0]),
                 (w_out_hbm, w_out),
             )
         )
@@ -136,13 +138,13 @@
 
     def ahead(slot):
         return (
-            lax.rem(grp + slot // n_head, n_grp),
+            lax.rem(grp + 2 * (slot // n_head), n_grp),
             lax.rem(head + slot % n_head, n_head),
         )
 
     def behind(slot):
         return (
-            lax.rem(grp + n_grp - slot // n_head, n_grp),
+            lax.rem(grp + n_grp - 2 * (slot // n_head), n_grp),
             lax.rem(head + n_head - slot % n_head, n_head),
         )
 
@@ -156,7 +158,10 @@
             barrier, inc=1, device_id=ahead(slot), device_id_type=MESH
         )
 
-    for_each(1, devices, greet)
+    for_each(1, peers, greet)
+    pl.semaphore_signal(
+        barrier, inc=1, device_id=(sibling, head), device_id_type=MESH
+    )
     for load in loads:
         load.start()
 
@@ -200,8 +205,18 @@
             device_id_type=MESH,
         )
 
-    pl.semaphore_wait(barrier, devices - 1)
-    for_each(1, devices, lambda slot: ask(slot).start())
+    swap = pltpu.make_async_remote_copy(
+        src_ref=new_cache_hbm,
+        dst_ref=new_cache.at[1],
+        send_sem=swap_sem.at[0],
+        recv_sem=swap_sem.at[1],
+        device_id=(sibling, head),
+        device_id_type=MESH,
+    )
+
+    pl.semaphore_wait(barrier, peers)
+    for_each(1, peers, lambda slot: ask(slot).start())
+    swap.start()
 
     token = lax.broadcasted_iota(jnp.int32, (1, residents * slots), 1)
     row = lax.broadcasted_iota(jnp.int32, (residents * heads, 1), 0) // heads
@@ -237,22 +252,25 @@
         [res_partial[:, i * piece : (i + 1) * piece] for i in range(splits)], axis=0
     ).astype(BF16)
 
-    first = (grp * n_head + head) * shard
     token = lax.broadcasted_iota(jnp.int32, (1, tokens), 1)
     asks = jnp.full((1, tokens), -1, jnp.int32)
     load_n.wait()
     load_a.wait()
-    for k in range(requests):
-        here = (token >= k * shard) & (token < k * shard + (new_lengths[k] - first))
-        here = here & (token < (k + 1) * shard)
-        asks = jnp.where(here, assignment[k], asks)
-    row = lax.broadcasted_iota(jnp.int32, (rows, 1), 0) // (heads * n_head)
+    for half, owner in enumerate((grp, sibling)):
+        first = (owner * n_head + head) * shard
+        for k in range(requests):
+            low = (half * requests + k) * shard
+            here = (token >= low) & (token < low + (new_lengths[k] - first))
+            here = here & (token < low + shard)
+            asks = jnp.where(here, assignment[k], asks)
+    row = lax.broadcasted_iota(jnp.int32, (rows, 1), 0) // (heads * n_head) * 2
     lane = lax.broadcasted_iota(jnp.int32, (rows, 128), 1)
     load_new.wait()
     load_q.wait()
+    swap.wait_recv()
 
     def attend_chunk(low):
-        group = grp - row - low // n_head
+        group = grp - row - low // n_head * 2
         group = jnp.where(group < 0, group + n_grp, group)
         top_hi, top_lo, total, weighted = attend(
             q_in[pl.ds(low, chunk)].astype(F32).reshape(rows, latent).astype(BF16),
@@ -272,12 +290,13 @@
             .astype(BF16)
         )
 
-    for_each(1, devices, lambda slot: ask(slot).wait_recv())
-    for_each(0, devices // chunk, lambda i: attend_chunk(i * chunk))
-    for_each(1, devices, lambda slot: answer(slot).start())
+    for_each(1, peers, lambda slot: ask(slot).wait_recv())
+    for_each(0, peers // chunk, lambda i: attend_chunk(i * chunk))
+    for_each(1, peers, lambda slot: answer(slot).start())
     for_each(1, n_head, lambda off: share_res(off).start())
     rep_in[0] = rep_out[0]
-    for_each(1, devices, lambda slot: ask(slot).wait_send())
+    for_each(1, peers, lambda slot: ask(slot).wait_send())
+    swap.wait_send()
 
     def add_chunk(low, so_far):
         parts = rep_in[pl.ds(low, chunk)].astype(F32)
@@ -297,11 +316,11 @@
             summed = summed + share * so_far[2]
         return top, total, summed
 
-    for_each(1, devices, lambda slot: answer(slot).wait_recv())
+    for_each(1, peers, lambda slot: answer(slot).wait_recv())
     sums = add_chunk(0, None)
-    if devices > chunk:
+    if peers > chunk:
         sums = lax.fori_loop(
-            1, devices // chunk, lambda i, so_far: add_chunk(i * chunk, so_far), sums
+            1, peers // chunk, lambda i, so_far: add_chunk(i * chunk, so_far), sums
         )
     _, total, summed = sums
     new_latent = (summed / total).astype(BF16)
@@ -310,7 +329,7 @@
     new_part[head] = jnp.dot(new_row, w_out[...], preferred_element_type=F32)
     for_each(1, n_head, lambda off: share_new(off).start())
 
-    for_each(1, devices, lambda slot: answer(slot).wait_send())
+    for_each(1, peers, lambda slot: answer(slot).wait_send())
     for_each(1, n_head, lambda off: share_res(off).wait_recv())
     res_sum = res_part[0].astype(F32)
     for rank in range(1, n_head):
@@ -328,17 +347,6 @@
     for_each(1, n_head, lambda off: share_new(off).wait_send())
 
 
-def write_back(res_in, new_in, res_out, new_out, sem):
-    copies = [
-        pltpu.make_async_copy(res_in, res_out, sem.at[0]),
-        pltpu.make_async_copy(new_in, new_out, sem.at[1]),
-    ]
-    for copy in copies:
-        copy.start()
-    for copy in copies:
-        copy.wait()
-
-
 def per_device(
     res_cache,
     res_lengths,
@@ -352,7 +360,7 @@
 ):
     n_grp = lax.axis_size("grp")
     n_head = lax.axis_size("head")
-    devices = n_grp * n_head
+    peers = n_grp // 2 * n_head
     residents = res_cache.shape[0]
     heads, width, head_width = value_up_weight.shape
     latent = res_cache.shape[2]
@@ -362,7 +370,7 @@
     hbm = pl.BlockSpec(memory_space=pltpu.HBM)
     vmem = pl.BlockSpec(memory_space=pltpu.VMEM)
     dma = pltpu.SemaphoreType.DMA
-    results = pl.pallas_call(
+    return pl.pallas_call(
         functools.partial(kernel, n_grp, n_head),
         out_shape=(
             pltpu.VMEM((residents, features), BF16),
@@ -376,17 +384,18 @@
             pltpu.SMEM(assignment.shape, jnp.int32),
             pltpu.VMEM(res_cache.shape, BF16),
             pltpu.VMEM(res_query.shape, BF16),
-            pltpu.VMEM(new_cache.shape, BF16),
+            pltpu.VMEM((2,) + new_cache.shape, BF16),
             pltpu.VMEM(value_up_weight.shape, BF16),
             pltpu.VMEM(w_out.shape, BF16),
-            pltpu.VMEM((devices, heads, latent), BF16),
-            pltpu.VMEM((devices, heads, width + 128), BF16),
-            pltpu.VMEM((devices, heads, width + 128), BF16),
+            pltpu.VMEM((peers, heads, latent), BF16),
+            pltpu.VMEM((peers, heads, width + 128), BF16),
+            pltpu.VMEM((peers, heads, width + 128), BF16),
             pltpu.VMEM((n_head, residents * splits, features // splits), BF16),
             pltpu.VMEM((n_head, 1, features), F32),
             dma((9,)),
+            dma((2,)),
         ]
-        + [dma((devices,))] * 4
+        + [dma((peers,))] * 4
         + [dma((n_head,))] * 4,
         compiler_params=pltpu.CompilerParams(
             collective_id=0, has_side_effects=True, vmem_limit_bytes=60 * 2**20
@@ -402,13 +411,6 @@
         value_up_weight,
         w_out,
     )
-    return pl.pallas_call(
-        write_back,
-        out_shape=tuple(jax.ShapeDtypeStruct(r.shape, r.dtype) for r in results),
-        in_specs=[vmem, vmem],
-        out_specs=(hbm, hbm),
-        scratch_shapes=[dma((2,))],
-    )(*results)
 
 
 def solution(mesh):

time: 28.9 us -> 24.4 us (0.84)
  Pallas kernels: 26.8 us -> 22.4 us
    pallas_call x1, Pallas kernels: 25.5 us -> 22.4 us  [per_device(): pl.pallas_call(functools.partial(kernel, n_grp, n_head), out_shape=(pltpu...]
    pallas_call x1 -> x0, Pallas kernels: 1.38 us -> none  [per_device(): pl.pallas_call(write_back, out_shape=tuple((jax.ShapeDtypeStruct(r.shape,...]
    unnamed x4 -> x2, local copies, waits for them, and re-layouts: 1.2 us -> 1.21 us
where the time goes in v4:
time: 24.4 us; the launch traced here: 24.3 us
  Pallas kernels  22.4 us (92%)
  local copies, waits for them, and re-layouts  1.21 us (5%)
  between operations  0.64 us (3%)
    pallas_call x1, Pallas kernels, per_device(): pl.pallas_call(functools.partial(kernel, n_grp, n_head), out_shape=(pltpu...  22.4 us
    unnamed x2, local copies, waits for them, and re-layouts  1.21 us

profile of v4, /device:TPU:0, one launch (start us, length us, event | category | flops | bytes accessed | tf_op | source)
XLA Modules:
  0.0 24.3 jit_solution(5729660708989156208)
XLA Ops:
  0.6 22.4 %shard_map.104 = (bf16[4,3584]{1,0:T(4,128)(2,1)S(1)}, bf16[1,3584]{1,0:T(2,128)(2,1)S(1)}) custom-call(s32[4]{0:T(128)} %res_lengths_hbm.1, s32[8]{0:T(128)} %new_lengths_hbm.1, s32[8]{0:T(128)} %assignment_hbm.1, bf16[4,576,128]{2,1,0:T(8,128)(2,1)} %bitcast.1, bf16[4,4,576]{2,1,0:T(4,128)(2,1)} %res_query_hbm.1, bf16[8,64,576]{2,1,0:T(8,128)(2,1)} %new_cache_hbm.1, ...), custom_call_target="tpu_custom_call" | custom-call | tf_op jit(solution)/shard_map/pallas_call | solution.py:373
  23.1 0.6 %copy.13 = bf16[4,3584]{1,0:T(4,128)(2,1)} copy(bf16[4,3584]{1,0:T(4,128)(2,1)S(1)} %get-tuple-element.2) | data formatting | bytes 57344
  23.7 0.6 %copy.14 = bf16[1,3584]{1,0:T(2,128)(2,1)} copy(bf16[1,3584]{1,0:T(2,128)(2,1)S(1)} %get-tuple-element.3) | data formatting | bytes 14336

commit v5 on v4

--- a/solution.py
+++ b/solution.py
@@ -215,7 +215,7 @@
     )
 
     pl.semaphore_wait(barrier, peers)
-    for_each(1, peers, lambda slot: ask(slot).start())
+    for_each(1, peers, lambda slot: ask(peers - slot).start())
     swap.start()
 
     token = lax.broadcasted_iota(jnp.int32, (1, residents * slots), 1)
@@ -246,11 +246,6 @@
     load_up.wait()
     res_values = up_project(res_latent, up, heads).astype(BF16).astype(F32)
     res_rows = flatten_heads(res_values, heads).astype(BF16)
-    load_w.wait()
-    res_partial = jnp.dot(res_rows, w_out[...], preferred_element_type=F32)
-    res_part[head] = jnp.concatenate(
-        [res_partial[:, i * piece : (i + 1) * piece] for i in range(splits)], axis=0
-    ).astype(BF16)
 
     token = lax.broadcasted_iota(jnp.int32, (1, tokens), 1)
     asks = jnp.full((1, tokens), -1, jnp.int32)
@@ -292,7 +287,12 @@
 
     for_each(1, peers, lambda slot: ask(slot).wait_recv())
     for_each(0, peers // chunk, lambda i: attend_chunk(i * chunk))
-    for_each(1, peers, lambda slot: answer(slot).start())
+    for_each(1, peers, lambda slot: answer(peers - slot).start())
+    load_w.wait()
+    res_partial = jnp.dot(res_rows, w_out[...], preferred_element_type=F32)
+    res_part[head] = jnp.concatenate(
+        [res_partial[:, i * piece : (i + 1) * piece] for i in range(splits)], axis=0
+    ).astype(BF16)
     for_each(1, n_head, lambda off: share_res(off).start())
     rep_in[0] = rep_out[0]
     for_each(1, peers, lambda slot: ask(slot).wait_send())

time: 24.4 us -> 23.4 us (0.959)
  Pallas kernels: 22.4 us -> 21.4 us
    pallas_call x1, Pallas kernels: 22.4 us -> 21.4 us  [per_device(): pl.pallas_call(functools.partial(kernel, n_grp, n_head), out_shape=(pltpu...]
where the time goes in v5:
time: 23.4 us; the launch traced here: 23.2 us
  Pallas kernels  21.4 us (91%)
  local copies, waits for them, and re-layouts  1.21 us (5%)
  between operations  0.64 us (3%)
    pallas_call x1, Pallas kernels, per_device(): pl.pallas_call(functools.partial(kernel, n_grp, n_head), out_shape=(pltpu...  21.4 us
    unnamed x2, local copies, waits for them, and re-layouts  1.21 us

profile of v5, /device:TPU:0, one launch (start us, length us, event | category | flops | bytes accessed | tf_op | source)
XLA Modules:
  0.0 23.2 jit_solution(10664228147248371992)
XLA Ops:
  0.6 21.4 %shard_map.104 = (bf16[4,3584]{1,0:T(4,128)(2,1)S(1)}, bf16[1,3584]{1,0:T(2,128)(2,1)S(1)}) custom-call(s32[4]{0:T(128)} %res_lengths_hbm.1, s32[8]{0:T(128)} %new_lengths_hbm.1, s32[8]{0:T(128)} %assignment_hbm.1, bf16[4,576,128]{2,1,0:T(8,128)(2,1)} %bitcast.1, bf16[4,4,576]{2,1,0:T(4,128)(2,1)} %res_query_hbm.1, bf16[8,64,576]{2,1,0:T(8,128)(2,1)} %new_cache_hbm.1, ...), custom_call_target="tpu_custom_call" | custom-call | tf_op jit(solution)/shard_map/pallas_call | solution.py:373
  22.0 0.6 %copy.13 = bf16[4,3584]{1,0:T(4,128)(2,1)} copy(bf16[4,3584]{1,0:T(4,128)(2,1)S(1)} %get-tuple-element.2) | data formatting | bytes 57344
  22.6 0.6 %copy.14 = bf16[1,3584]{1,0:T(2,128)(2,1)} copy(bf16[1,3584]{1,0:T(2,128)(2,1)S(1)} %get-tuple-element.3) | data formatting | bytes 14336

commit v6 on v5

--- a/solution.py
+++ b/solution.py
@@ -158,7 +158,7 @@
             barrier, inc=1, device_id=ahead(slot), device_id_type=MESH
         )
 
-    for_each(1, peers, greet)
+    for_each(1, peers, lambda slot: greet(peers - slot))
     pl.semaphore_signal(
         barrier, inc=1, device_id=(sibling, head), device_id_type=MESH
     )
@@ -327,7 +327,7 @@
     new_values = up_project(new_latent, up, heads).astype(BF16).astype(F32)
     new_row = flatten_heads(new_values, heads).astype(BF16)
     new_part[head] = jnp.dot(new_row, w_out[...], preferred_element_type=F32)
-    for_each(1, n_head, lambda off: share_new(off).start())
+    for_each(1, n_head, lambda off: share_new(n_head - off).start())
 
     for_each(1, peers, lambda slot: answer(slot).wait_send())
     for_each(1, n_head, lambda off: share_res(off).wait_recv())

time: 23.4 us -> 23.5 us (level)
  no operation moved by 1% of the time
where the time goes in v6:
time: 23.5 us; the launch traced here: 23.3 us
  Pallas kernels  21.5 us (91%)
  local copies, waits for them, and re-layouts  1.21 us (5%)
  between operations  0.64 us (3%)
    pallas_call x1, Pallas kernels, per_device(): pl.pallas_call(functools.partial(kernel, n_grp, n_head), out_shape=(pltpu...  21.5 us
    unnamed x2, local copies, waits for them, and re-layouts  1.21 us

profile of v6, /device:TPU:0, one launch (start us, length us, event | category | flops | bytes accessed | tf_op | source)
XLA Modules:
  0.0 23.3 jit_solution(7854616624426440493)
XLA Ops:
  0.6 21.5 %shard_map.104 = (bf16[4,3584]{1,0:T(4,128)(2,1)S(1)}, bf16[1,3584]{1,0:T(2,128)(2,1)S(1)}) custom-call(s32[4]{0:T(128)} %res_lengths_hbm.1, s32[8]{0:T(128)} %new_lengths_hbm.1, s32[8]{0:T(128)} %assignment_hbm.1, bf16[4,576,128]{2,1,0:T(8,128)(2,1)} %bitcast.1, bf16[4,4,576]{2,1,0:T(4,128)(2,1)} %res_query_hbm.1, bf16[8,64,576]{2,1,0:T(8,128)(2,1)} %new_cache_hbm.1, ...), custom_call_target="tpu_custom_call" | custom-call | tf_op jit(solution)/shard_map/pallas_call | solution.py:373
  22.1 0.6 %copy.13 = bf16[4,3584]{1,0:T(4,128)(2,1)} copy(bf16[4,3584]{1,0:T(4,128)(2,1)S(1)} %get-tuple-element.2) | data formatting | bytes 57344
  22.7 0.6 %copy.14 = bf16[1,3584]{1,0:T(2,128)(2,1)} copy(bf16[1,3584]{1,0:T(2,128)(2,1)S(1)} %get-tuple-element.3) | data formatting | bytes 14336
